TPU v7x, 32 devices: a whole 2x2x4 slice. The times are simulated.
32 devices in a mesh: sec: 2 (over x), az: 16 (over z, y, core).
Axes of the slice: x: 2, y: 2, z: 4, core: 2. Of those that a mesh axis runs over, the one named last changes fastest.
Arguments:
- axial: float32 [2, 4, 128, 1024], P('sec', None, 'az'), may hold values from -6 to 6
- azimuthal: float32 [2, 4, 128, 1024], P('sec', None, 'az'), may hold values from -6 to 6
- radial: float32 [2, 4, 128, 1024], P('sec', None, 'az'), may hold values from -6 to 6
- drag_blocks: int32 [2, 128, 16], P('sec', 'az'), may hold values 0 or 1
- rotation: int32 [1], replicated, may hold values from 1 to 15
- row_pairs: int32 [8], replicated, may hold values from 0 to 7, each once
Outputs:
- axial_out: float32 [2, 4, 128, 1024], P('sec', None, 'az')
- azimuthal_out: float32 [2, 4, 128, 1024], P('sec', None, 'az')
- radial_out: float32 [2, 4, 128, 1024], P('sec', None, 'az')
Inputs may be any that keep to these rules, and one draw needn't show every extreme that they name: rotation is a whole number of azimuthal blocks. row_pairs holds each of 0 to 7 once.
All inputs are finite; a program needn't handle non-finite values. No bound on the sum of `drag_blocks` on one device may be relied on, other than what follows from the above.
Results may differ from a plain program's by a relative error of at most 0.0001.
Values sent between devices are 32-bit elements; how exact they have to be, the bound alone decides.
A program may use at most 64 MiB of HBM per device.

v0:
```python
import jax
import jax.numpy as jnp
from jax import lax
from jax.sharding import PartitionSpec as P

STEPS = 2
ITERS = 3


courant = 0.5
viscosity = 0.1
diagonal_add = 0.05
drag_rate = 2.0
block_cells = 64


def extended(cells, sides, width):
    for axis, dim in sides:
        count = lax.axis_size(axis)
        head = lax.slice_in_dim(cells, 0, width, axis=dim)
        tail = lax.slice_in_dim(cells, cells.shape[dim] - width, cells.shape[dim], axis=dim)
        cells = jnp.concatenate(
            [
                lax.ppermute(tail, axis, [(i, (i + 1) % count) for i in range(count)]),
                cells,
                lax.ppermute(head, axis, [((i + 1) % count, i) for i in range(count)]),
            ],
            axis=dim,
        )
    return cells


def passed_along(block, axis, distance):
    devices = range(lax.axis_size(axis))
    route = [(i - distance, i) for i in devices if i - distance in devices]
    return lax.ppermute(block, axis, route)


def from_behind(array, axis, by):
    length = lax.axis_size(axis)
    return lax.ppermute(array, axis, [(i, (i + by) % length) for i in range(length)])


def widen_rows(stack):
    return extended(stack, (("az", 2),), 1)


def neighbours(widened):
    inner = widened[:, :, 1:-1]
    padded = jnp.pad(inner, ((0, 0), (0, 0), (0, 0), (1, 1)))
    return widened[:, :, 2:] + widened[:, :, :-2] + padded[..., 2:] + padded[..., :-2]


def operate(field, diag_coef):
    widened = widen_rows(field[None])
    return diag_coef * field - neighbours(widened)[0]


def local_sums(values):
    return jnp.sum(values, axis=(1, 2), keepdims=True)


def paired_products(residual, applied):
    return lax.psum((local_sums(residual * residual), local_sums(residual * applied)), "az")


def solve(source, diag_coef):
    solution = jnp.zeros_like(source)
    residual = source
    applied = operate(residual, diag_coef)
    norm_now, product = paired_products(residual, applied)
    step_size = norm_now / product
    direction = residual
    along = applied
    for iteration in range(ITERS):
        solution = solution + step_size * direction
        residual = residual - step_size * along
        if iteration + 1 < ITERS:
            applied = operate(residual, diag_coef)
            norm_next, product = paired_products(residual, applied)
            beta_ratio = norm_next / norm_now
            step_size = norm_next / (product - beta_ratio * norm_next / step_size)
            direction = residual + beta_ratio * direction
            along = applied + beta_ratio * along
            norm_now = norm_next
    return solution


def advance(fields, upstream_plane, diag_coef):
    widened = widen_rows(fields)
    upstream = jnp.concatenate([upstream_plane[:, None], fields[:, :-1]], axis=1)
    predicted = (
        fields - courant * (fields - upstream) + viscosity * (neighbours(widened) - 4.0 * fields)
    )
    azimuth_prev = widen_rows(predicted[1:2])[0, :, :-2]
    azimuth_vel = predicted[1]
    radial_vel = predicted[2]
    radial_prev = jnp.pad(radial_vel, ((0, 0), (0, 0), (1, 0)))[..., :-1]
    divergence = azimuth_vel - azimuth_prev + (radial_vel - radial_prev)
    pressure = solve(divergence, diag_coef)
    widened_press = widen_rows(pressure[None])[0]
    next_azimuth = widened_press[:, 2:]
    next_radial = jnp.pad(pressure, ((0, 0), (0, 0), (0, 1)))[..., 1:]
    return jnp.stack(
        [
            predicted[0],
            azimuth_vel - (next_azimuth - pressure),
            radial_vel - (next_radial - pressure),
        ]
    )


def body(axial, azimuthal, radial, drag_blocks, rotation, row_pairs):
    fields = jnp.stack([axial[0], azimuthal[0], radial[0]])
    sleeve_side = lax.axis_index("sec") == 1
    drag_map = jnp.repeat(drag_blocks[0].astype(jnp.float32), block_cells, axis=1)
    diag_coef = 4.0 + diagonal_add + drag_rate * drag_map
    cycle_size = lax.axis_size("az")
    for time_step in range(STEPS):
        outlet = fields[:, -1]
        across = passed_along(outlet, "sec", 1)
        turn_blocks = rotation[0] * (time_step + 1) % cycle_size
        moved = across
        for bit_index in range((cycle_size - 1).bit_length()):
            turned = from_behind(moved, "az", 1 << bit_index)
            moved = jnp.where(turn_blocks // (1 << bit_index) % 2 == 1, turned, moved)
        inflow = jnp.take(moved, row_pairs, axis=1)
        upstream_plane = jnp.where(sleeve_side, inflow, outlet)
        fields = advance(fields, upstream_plane, diag_coef)
    return (fields[0][None], fields[1][None], fields[2][None])


def solution(mesh):
    in_specs = (
        P("sec", None, "az", None),
        P("sec", None, "az", None),
        P("sec", None, "az", None),
        P("sec", "az", None),
        P(),
        P(),
    )
    out_specs = (P("sec", None, "az", None), P("sec", None, "az", None), P("sec", None, "az", None))
    return jax.shard_map(body, mesh=mesh, in_specs=in_specs, out_specs=out_specs, check_vma=False)
```

profile of v0, /device:TPU:3, one launch (start us, length us, event | category | flops | bytes accessed | tf_op | source)
XLA Modules:
  0.0 308.3 jit_solution(2468352297607560811)
XLA Ops:
  0.6 0.9 constant_dynamic-update-slice_fusion.2
  1.6 0.9 copy-done.1
  2.5 1.3 collective-permute-start
  3.8 4.1 %collective-permute-done = f32[3,8,1024]{2,1,0:T(8,128)S(1)} collective-permute-done((f32[3,8,1024]{2,1,0:T(8,128)S(1)}, f32[3,8,1024]{2,1,0:T(8,128)S(1)}, u32[]{:S(2)}, u32[]{:S(2)}) %collective-permute-start) | collective-permute-done | bytes 98336 | tf_op jit(solution)/shard_map/ppermute | solution.py:36
  7.9 2.9 collective-permute-start.1
  11.0 1.7 collective-permute-start.6
  13.4 2.2 collective-permute-start.2
  15.7 5.4 %collective-permute-done.2 = f32[3,8,1024]{2,1,0:T(8,128)S(1)} collective-permute-done((f32[3,8,1024]{2,1,0:T(8,128)S(1)}, f32[3,8,1024]{2,1,0:T(8,128)S(1)}, u32[]{:S(2)}, u32[]{:S(2)}) %collective-permute-start.2) | collective-permute-done | bytes 98336 | tf_op jit(solution)/shard_map/ppermute | solution.py:41
  21.3 5.1 %collective-permute-done.3 = f32[3,8,1024]{2,1,0:T(8,128)S(1)} collective-permute-done((f32[3,8,1024]{2,1,0:T(8,128)S(1)}, f32[3,8,1024]{2,1,0:T(8,128)S(1)}, u32[]{:S(2)}, u32[]{:S(2)}) %collective-permute-start.3) | collective-permute-done | bytes 98336 | tf_op jit(solution)/shard_map/ppermute | solution.py:41
  26.6 4.4 %collective-permute-done.4 = f32[3,8,1024]{2,1,0:T(8,128)S(1)} collective-permute-done((f32[3,8,1024]{2,1,0:T(8,128)S(1)}, f32[3,8,1024]{2,1,0:T(8,128)S(1)}, u32[]{:S(2)}, u32[]{:S(2)}) %collective-permute-start.4) | collective-permute-done | bytes 98336 | tf_op jit(solution)/shard_map/ppermute | solution.py:41
  31.0 0.6 gather_fusion
  31.8 0.4 fusion.4
  32.1 2.6 collective-permute-start.7
  34.8 3.3 %collective-permute-done.7 = f32[1,4,1,1024]{3,2,1,0:T(1,128)S(1)} collective-permute-done((f32[1,4,1,1024]{3,2,1,0:T(1,128)S(1)}, f32[1,4,1,1024]{3,2,1,0:T(1,128)S(1)}, u32[]{:S(2)}, u32[]{:S(2)}) %collective-permute-start.7) | collective-permute-done | bytes 16416 | tf_op jit(solution)/shard_map/ppermute | solution.py:24
  38.3 5.2 %collective-permute-start.8 = (f32[1,4,1,1024]{3,2,1,0:T(1,128)S(1)}, f32[1,4,1,1024]{3,2,1,0:T(1,128)S(1)}, u32[]{:S(2)}, u32[]{:S(2)}) collective-permute-start(f32[1,4,1,1024]{3,2,1,0:T(1,128)S(1)} %get-tuple-element.68), channel_id=1, source_target_pairs={{1,0},{2,1},{3,2},{4,3},{5,4},{6,5},{7,6},{8,7},{9,8},{10,9},{11,1... | collective-permute-start | bytes 49160 | tf_op jit(solution)/shard_map/ppermute | solution.py:26
  43.7 0.7 collective-permute-done.8
  44.3 0.3 collective-permute-done.9
  44.7 0.2 multiply_reduce_fusion.8
  44.9 33.6 %all-reduce.17 = (f32[4,1,1]{0,2,1:T(1,128)S(1)}, f32[4,1,1]{0,2,1:T(1,128)S(1)}) all-reduce(f32[4,1,1]{0,2,1:T(1,128)S(1)} %bitcast.174, f32[4,1,1]{0,2,1:T(1,128)S(1)} %bitcast.173), channel_id=1, replica_groups=mesh['sec'=2,'az'=16] {'az'}, use_global_device_ids=true, to_apply=%region_1.3 | all-reduce | flops 8 | bytes 64 | tf_op jit(solution)/shard_map/psum | solution.py:64
  78.6 0.7 collective-permute-start.10
  79.3 1.1 collective-permute-start.11
  80.4 1.4 collective-permute-done.10
  81.8 0.2 multiply_reduce_fusion.6
  82.1 32.2 %all-reduce.16 = (f32[4,1,1]{0,2,1:T(1,128)S(1)}, f32[4,1,1]{0,2,1:T(1,128)S(1)}) all-reduce(f32[4,1,1]{0,2,1:T(1,128)S(1)} %bitcast.182, f32[4,1,1]{0,2,1:T(1,128)S(1)} %bitcast.181), channel_id=1, replica_groups=mesh['sec'=2,'az'=16] {'az'}, use_global_device_ids=true, to_apply=%region_5.7 | all-reduce | flops 8 | bytes 64 | tf_op jit(solution)/shard_map/psum | solution.py:64
  114.5 0.7 collective-permute-start.12
  115.2 1.1 collective-permute-start.13
  116.3 1.4 collective-permute-done.12
  117.7 0.2 fusion.29
  118.0 32.2 %all-reduce.15 = (f32[4,1,1]{0,2,1:T(1,128)S(1)}, f32[4,1,1]{0,2,1:T(1,128)S(1)}) all-reduce(f32[4,1,1]{0,2,1:T(1,128)S(1)} %bitcast.180, f32[4,1,1]{0,2,1:T(1,128)S(1)} %bitcast.179), channel_id=1, replica_groups=mesh['sec'=2,'az'=16] {'az'}, use_global_device_ids=true, to_apply=%region_9.11 | all-reduce | flops 8 | bytes 64 | tf_op jit(solution)/shard_map/psum | solution.py:64
  150.5 0.7 collective-permute-start.15
  151.2 0.6 collective-permute-done.14
  151.8 1.9 collective-permute-done.15
  153.9 1.3 collective-permute-start.16
  155.2 4.1 %collective-permute-done.16 = f32[3,8,1024]{2,1,0:T(8,128)S(1)} collective-permute-done((f32[3,8,1024]{2,1,0:T(8,128)S(1)}, f32[3,8,1024]{2,1,0:T(8,128)S(1)}, u32[]{:S(2)}, u32[]{:S(2)}) %collective-permute-start.16) | collective-permute-done | bytes 98336 | tf_op jit(solution)/shard_map/ppermute | solution.py:36
  159.2 1.2 collective-permute-start.17
  160.4 4.1 %collective-permute-done.17 = f32[3,8,1024]{2,1,0:T(8,128)S(1)} collective-permute-done((f32[3,8,1024]{2,1,0:T(8,128)S(1)}, f32[3,8,1024]{2,1,0:T(8,128)S(1)}, u32[]{:S(2)}, u32[]{:S(2)}) %collective-permute-start.17) | collective-permute-done | bytes 98336 | tf_op jit(solution)/shard_map/ppermute | solution.py:41
  164.6 6.8 %collective-permute-done.18 = f32[3,8,1024]{2,1,0:T(8,128)S(1)} collective-permute-done((f32[3,8,1024]{2,1,0:T(8,128)S(1)}, f32[3,8,1024]{2,1,0:T(8,128)S(1)}, u32[]{:S(2)}, u32[]{:S(2)}) %collective-permute-start.18) | collective-permute-done | bytes 98336 | tf_op jit(solution)/shard_map/ppermute | solution.py:41
  171.6 5.5 %collective-permute-done.19 = f32[3,8,1024]{2,1,0:T(8,128)S(1)} collective-permute-done((f32[3,8,1024]{2,1,0:T(8,128)S(1)}, f32[3,8,1024]{2,1,0:T(8,128)S(1)}, u32[]{:S(2)}, u32[]{:S(2)}) %collective-permute-start.19) | collective-permute-done | bytes 98336 | tf_op jit(solution)/shard_map/ppermute | solution.py:41
  177.3 7.3 %collective-permute-start.21 = (f32[3,4,1,1024]{3,2,1,0:T(1,128)S(1)}, f32[3,4,1,1024]{3,2,1,0:T(1,128)S(1)}, u32[]{:S(2)}, u32[]{:S(2)}) collective-permute-start(f32[3,4,1,1024]{3,2,1,0:T(1,128)S(1)} %get-tuple-element.47), channel_id=1, source_target_pairs={{1,0},{2,1},{3,2},{4,3},{5,4},{6,5},{7,6},{8,7},{9,8},{10,9},{11,1... | collective-permute-start | bytes 147464 | tf_op jit(solution)/shard_map/ppermute | solution.py:26
  184.7 0.6 gather_fusion.1
  185.4 0.5 collective-permute-done.22
  185.9 0.4 fusion.9
  186.3 2.5 collective-permute-start.23
  188.8 0.7 fusion.74
  189.5 2.4 collective-permute-done.23
  192.1 5.2 %collective-permute-start.24 = (f32[1,4,1,1024]{3,2,1,0:T(1,128)S(1)}, f32[1,4,1,1024]{3,2,1,0:T(1,128)S(1)}, u32[]{:S(2)}, u32[]{:S(2)}) collective-permute-start(f32[1,4,1,1024]{3,2,1,0:T(1,128)S(1)} %get-tuple-element.60), channel_id=1, source_target_pairs={{1,0},{2,1},{3,2},{4,3},{5,4},{6,5},{7,6},{8,7},{9,8},{10,9},{11,1... | collective-permute-start | bytes 49160 | tf_op jit(solution)/shard_map/ppermute | solution.py:26
  197.3 0.8 collective-permute-done.24
  198.2 0.3 collective-permute-done.25
  198.5 0.2 multiply_reduce_fusion.3
  198.7 33.6 %all-reduce.14 = (f32[4,1,1]{0,2,1:T(1,128)S(1)}, f32[4,1,1]{0,2,1:T(1,128)S(1)}) all-reduce(f32[4,1,1]{0,2,1:T(1,128)S(1)} %bitcast.176, f32[4,1,1]{0,2,1:T(1,128)S(1)} %bitcast.175), channel_id=1, replica_groups=mesh['sec'=2,'az'=16] {'az'}, use_global_device_ids=true, to_apply=%region_13.15 | all-reduce | flops 8 | bytes 64 | tf_op jit(solution)/shard_map/psum | solution.py:64
  232.4 0.7 collective-permute-start.26
  233.1 1.1 collective-permute-start.27
  234.2 1.4 collective-permute-done.26
  235.7 0.2 multiply_reduce_fusion.1
  235.9 32.2 %all-reduce.13 = (f32[4,1,1]{0,2,1:T(1,128)S(1)}, f32[4,1,1]{0,2,1:T(1,128)S(1)}) all-reduce(f32[4,1,1]{0,2,1:T(1,128)S(1)} %bitcast.184, f32[4,1,1]{0,2,1:T(1,128)S(1)} %bitcast.183), channel_id=1, replica_groups=mesh['sec'=2,'az'=16] {'az'}, use_global_device_ids=true, to_apply=%region_17.19 | all-reduce | flops 8 | bytes 64 | tf_op jit(solution)/shard_map/psum | solution.py:64
  268.3 0.7 collective-permute-start.28
  269.0 1.1 collective-permute-start.29
  270.1 1.4 collective-permute-done.28
  271.6 0.2 fusion.43
  271.8 32.2 %all-reduce.12 = (f32[4,1,1]{0,2,1:T(1,128)S(1)}, f32[4,1,1]{0,2,1:T(1,128)S(1)}) all-reduce(f32[4,1,1]{0,2,1:T(1,128)S(1)} %bitcast.178, f32[4,1,1]{0,2,1:T(1,128)S(1)} %bitcast.177), channel_id=1, replica_groups=mesh['sec'=2,'az'=16] {'az'}, use_global_device_ids=true, to_apply=%region_21.23 | all-reduce | flops 8 | bytes 64 | tf_op jit(solution)/shard_map/psum | solution.py:64
  304.3 0.7 collective-permute-start.31
  305.0 0.6 collective-permute-done.30
  305.6 1.9 collective-permute-done.31
  307.5 0.8 fusion.53
  (82 shorter events, 2.9 us)
Async XLA Ops:
  0.6 1.0 copy-start
  1.6 0.9 copy-start.1
  2.5 5.4 %collective-permute-start = (f32[3,8,1024]{2,1,0:T(8,128)S(1)}, f32[3,8,1024]{2,1,0:T(8,128)S(1)}, u32[]{:S(2)}, u32[]{:S(2)}) collective-permute-start(f32[3,8,1024]{2,1,0:T(8,128)S(1)} %slice_bitcast_fusion.3), channel_id=1, source_target_pairs={{0,16},{1,17},{2,18},{3,19},{4,20},{5,21},{6,22},{7,23},{8,24},{9,... | collective-permute-start | bytes 294920 | tf_op jit(solution)/shard_map/ppermute | solution.py:36
  7.9 5.5 %collective-permute-start.1 = (f32[3,8,1024]{2,1,0:T(8,128)S(1)}, f32[3,8,1024]{2,1,0:T(8,128)S(1)}, u32[]{:S(2)}, u32[]{:S(2)}) collective-permute-start(f32[3,8,1024]{2,1,0:T(8,128)S(1)} %collective-permute-done), channel_id=1, source_target_pairs={{0,1},{1,2},{2,3},{3,4},{4,5},{5,6},{6,7},{7,8},{8,9},{9,10},{10,1... | collective-permute-start | bytes 294920 | tf_op jit(solution)/shard_map/ppermute | solution.py:41
  10.9 20.8 %collective-permute-start.5 = (f32[3,4,1,1024]{3,2,1,0:T(1,128)S(1)}, f32[3,4,1,1024]{3,2,1,0:T(1,128)S(1)}, u32[]{:S(2)}, u32[]{:S(2)}) collective-permute-start(f32[3,4,1,1024]{3,2,1,0:T(1,128)S(1)} %get-tuple-element.52), channel_id=1, source_target_pairs={{1,0},{2,1},{3,2},{4,3},{5,4},{6,5},{7,6},{8,7},{9,8},{10,9},{11,1... | collective-permute-start | bytes 147464 | tf_op jit(solution)/shard_map/ppermute | solution.py:26
  11.0 20.8 %collective-permute-start.6 = (f32[3,4,1,1024]{3,2,1,0:T(1,128)S(1)}, f32[3,4,1,1024]{3,2,1,0:T(1,128)S(1)}, u32[]{:S(2)}, u32[]{:S(2)}) collective-permute-start(f32[3,4,1,1024]{3,2,1,0:T(1,128)S(1)} %get-tuple-element.53), channel_id=1, source_target_pairs={{0,1},{1,2},{2,3},{3,4},{4,5},{5,6},{6,7},{7,8},{8,9},{9,10},{10,1... | collective-permute-start | bytes 147464 | tf_op jit(solution)/shard_map/ppermute | solution.py:24
  13.4 2.2 copy-start.3
  13.4 7.7 %collective-permute-start.2 = (f32[3,8,1024]{2,1,0:T(8,128)S(1)}, f32[3,8,1024]{2,1,0:T(8,128)S(1)}, u32[]{:S(2)}, u32[]{:S(2)}) collective-permute-start(f32[3,8,1024]{2,1,0:T(8,128)S(1)} %broadcast_select_fusion.4), channel_id=1, source_target_pairs={{0,2},{1,3},{2,4},{3,5},{4,6},{5,7},{6,8},{7,9},{8,10},{9,11},{10,... | collective-permute-start | bytes 294920 | tf_op jit(solution)/shard_map/ppermute | solution.py:41
  21.1 5.3 %collective-permute-start.3 = (f32[3,8,1024]{2,1,0:T(8,128)S(1)}, f32[3,8,1024]{2,1,0:T(8,128)S(1)}, u32[]{:S(2)}, u32[]{:S(2)}) collective-permute-start(f32[3,8,1024]{2,1,0:T(8,128)S(1)} %broadcast_select_fusion.5), channel_id=1, source_target_pairs={{0,4},{1,5},{2,6},{3,7},{4,8},{5,9},{6,10},{7,11},{8,12},{9,13},{1... | collective-permute-start | bytes 294920 | tf_op jit(solution)/shard_map/ppermute | solution.py:41
  26.5 4.5 %collective-permute-start.4 = (f32[3,8,1024]{2,1,0:T(8,128)S(1)}, f32[3,8,1024]{2,1,0:T(8,128)S(1)}, u32[]{:S(2)}, u32[]{:S(2)}) collective-permute-start(f32[3,8,1024]{2,1,0:T(8,128)S(1)} %broadcast_select_fusion.6), channel_id=1, source_target_pairs={{0,8},{1,9},{2,10},{3,11},{4,12},{5,13},{6,14},{7,15},{8,0},{9,1},... | collective-permute-start | bytes 294920 | tf_op jit(solution)/shard_map/ppermute | solution.py:41
  32.1 6.0 %collective-permute-start.7 = (f32[1,4,1,1024]{3,2,1,0:T(1,128)S(1)}, f32[1,4,1,1024]{3,2,1,0:T(1,128)S(1)}, u32[]{:S(2)}, u32[]{:S(2)}) collective-permute-start(f32[1,4,1,1024]{3,2,1,0:T(1,128)S(1)} %slice.320), channel_id=1, source_target_pairs={{0,1},{1,2},{2,3},{3,4},{4,5},{5,6},{6,7},{7,8},{8,9},{9,10},{10,1... | collective-permute-start | bytes 49160 | tf_op jit(solution)/shard_map/ppermute | solution.py:24
  38.2 5.3 %copy-start.2 = (s32[1,8,16]{2,1,0:T(8,128)S(1)}, s32[1,8,16]{2,1,0:T(8,128)}, u32[]{:S(2)}) copy-start(s32[1,8,16]{2,1,0:T(8,128)} %param.11) | copy-start | bytes 1540
  38.3 6.1 %collective-permute-start.8 = (f32[1,4,1,1024]{3,2,1,0:T(1,128)S(1)}, f32[1,4,1,1024]{3,2,1,0:T(1,128)S(1)}, u32[]{:S(2)}, u32[]{:S(2)}) collective-permute-start(f32[1,4,1,1024]{3,2,1,0:T(1,128)S(1)} %get-tuple-element.68), channel_id=1, source_target_pairs={{1,0},{2,1},{3,2},{4,3},{5,4},{6,5},{7,6},{8,7},{9,8},{10,9},{11,1... | collective-permute-start | bytes 49160 | tf_op jit(solution)/shard_map/ppermute | solution.py:26
  43.5 1.2 collective-permute-start.9
  78.6 3.2 %collective-permute-start.10 = (f32[1,4,1,1024]{3,2,1,0:T(1,128)S(1)}, f32[1,4,1,1024]{3,2,1,0:T(1,128)S(1)}, u32[]{:S(2)}, u32[]{:S(2)}) collective-permute-start(f32[1,4,1,1024]{3,2,1,0:T(1,128)S(1)} %get-tuple-element.66), channel_id=1, source_target_pairs={{1,0},{2,1},{3,2},{4,3},{5,4},{6,5},{7,6},{8,7},{9,8},{10,9},{11,1... | collective-permute-start | bytes 49160 | tf_op jit(solution)/shard_map/ppermute | solution.py:26
  79.3 2.5 collective-permute-start.11
  114.5 3.2 %collective-permute-start.12 = (f32[1,4,1,1024]{3,2,1,0:T(1,128)S(1)}, f32[1,4,1,1024]{3,2,1,0:T(1,128)S(1)}, u32[]{:S(2)}, u32[]{:S(2)}) collective-permute-start(f32[1,4,1,1024]{3,2,1,0:T(1,128)S(1)} %get-tuple-element.64), channel_id=1, source_target_pairs={{1,0},{2,1},{3,2},{4,3},{5,4},{6,5},{7,6},{8,7},{9,8},{10,9},{11,1... | collective-permute-start | bytes 49160 | tf_op jit(solution)/shard_map/ppermute | solution.py:26
  115.2 2.5 collective-permute-start.13
  150.4 1.4 collective-permute-start.14
  150.5 3.2 %collective-permute-start.15 = (f32[1,4,1,1024]{3,2,1,0:T(1,128)S(1)}, f32[1,4,1,1024]{3,2,1,0:T(1,128)S(1)}, u32[]{:S(2)}, u32[]{:S(2)}) collective-permute-start(f32[1,4,1,1024]{3,2,1,0:T(1,128)S(1)} %get-tuple-element.63), channel_id=1, source_target_pairs={{1,0},{2,1},{3,2},{4,3},{5,4},{6,5},{7,6},{8,7},{9,8},{10,9},{11,1... | collective-permute-start | bytes 49160 | tf_op jit(solution)/shard_map/ppermute | solution.py:26
  153.9 5.4 %collective-permute-start.16 = (f32[3,8,1024]{2,1,0:T(8,128)S(1)}, f32[3,8,1024]{2,1,0:T(8,128)S(1)}, u32[]{:S(2)}, u32[]{:S(2)}) collective-permute-start(f32[3,8,1024]{2,1,0:T(8,128)S(1)} %slice_bitcast_fusion.2), channel_id=1, source_target_pairs={{0,16},{1,17},{2,18},{3,19},{4,20},{5,21},{6,22},{7,23},{8,24},{9,... | collective-permute-start | bytes 294920 | tf_op jit(solution)/shard_map/ppermute | solution.py:36
  159.2 5.2 %collective-permute-start.17 = (f32[3,8,1024]{2,1,0:T(8,128)S(1)}, f32[3,8,1024]{2,1,0:T(8,128)S(1)}, u32[]{:S(2)}, u32[]{:S(2)}) collective-permute-start(f32[3,8,1024]{2,1,0:T(8,128)S(1)} %collective-permute-done.16), channel_id=1, source_target_pairs={{0,1},{1,2},{2,3},{3,4},{4,5},{5,6},{6,7},{7,8},{8,9},{9,10},{10,1... | collective-permute-start | bytes 294920 | tf_op jit(solution)/shard_map/ppermute | solution.py:41
  164.5 7.0 %collective-permute-start.18 = (f32[3,8,1024]{2,1,0:T(8,128)S(1)}, f32[3,8,1024]{2,1,0:T(8,128)S(1)}, u32[]{:S(2)}, u32[]{:S(2)}) collective-permute-start(f32[3,8,1024]{2,1,0:T(8,128)S(1)} %broadcast_select_fusion), channel_id=1, source_target_pairs={{0,2},{1,3},{2,4},{3,5},{4,6},{5,7},{6,8},{7,9},{8,10},{9,11},{10,... | collective-permute-start | bytes 294920 | tf_op jit(solution)/shard_map/ppermute | solution.py:41
  171.5 5.6 %collective-permute-start.19 = (f32[3,8,1024]{2,1,0:T(8,128)S(1)}, f32[3,8,1024]{2,1,0:T(8,128)S(1)}, u32[]{:S(2)}, u32[]{:S(2)}) collective-permute-start(f32[3,8,1024]{2,1,0:T(8,128)S(1)} %broadcast_select_fusion.1), channel_id=1, source_target_pairs={{0,4},{1,5},{2,6},{3,7},{4,8},{5,9},{6,10},{7,11},{8,12},{9,13},{1... | collective-permute-start | bytes 294920 | tf_op jit(solution)/shard_map/ppermute | solution.py:41
  177.1 7.4 %collective-permute-start.20 = (f32[3,8,1024]{2,1,0:T(8,128)S(1)}, f32[3,8,1024]{2,1,0:T(8,128)S(1)}, u32[]{:S(2)}, u32[]{:S(2)}) collective-permute-start(f32[3,8,1024]{2,1,0:T(8,128)S(1)} %broadcast_select_fusion.2), channel_id=1, source_target_pairs={{0,8},{1,9},{2,10},{3,11},{4,12},{5,13},{6,14},{7,15},{8,0},{9,1},... | collective-permute-start | bytes 294920 | tf_op jit(solution)/shard_map/ppermute | solution.py:41
  177.3 8.1 %collective-permute-start.21 = (f32[3,4,1,1024]{3,2,1,0:T(1,128)S(1)}, f32[3,4,1,1024]{3,2,1,0:T(1,128)S(1)}, u32[]{:S(2)}, u32[]{:S(2)}) collective-permute-start(f32[3,4,1,1024]{3,2,1,0:T(1,128)S(1)} %get-tuple-element.47), channel_id=1, source_target_pairs={{1,0},{2,1},{3,2},{4,3},{5,4},{6,5},{7,6},{8,7},{9,8},{10,9},{11,1... | collective-permute-start | bytes 147464 | tf_op jit(solution)/shard_map/ppermute | solution.py:26
  184.6 1.4 collective-permute-start.22
  186.3 5.7 %collective-permute-start.23 = (f32[1,4,1,1024]{3,2,1,0:T(1,128)S(1)}, f32[1,4,1,1024]{3,2,1,0:T(1,128)S(1)}, u32[]{:S(2)}, u32[]{:S(2)}) collective-permute-start(f32[1,4,1,1024]{3,2,1,0:T(1,128)S(1)} %slice.337), channel_id=1, source_target_pairs={{0,1},{1,2},{2,3},{3,4},{4,5},{5,6},{6,7},{7,8},{8,9},{9,10},{10,1... | collective-permute-start | bytes 49160 | tf_op jit(solution)/shard_map/ppermute | solution.py:24
  192.1 6.1 %collective-permute-start.24 = (f32[1,4,1,1024]{3,2,1,0:T(1,128)S(1)}, f32[1,4,1,1024]{3,2,1,0:T(1,128)S(1)}, u32[]{:S(2)}, u32[]{:S(2)}) collective-permute-start(f32[1,4,1,1024]{3,2,1,0:T(1,128)S(1)} %get-tuple-element.60), channel_id=1, source_target_pairs={{1,0},{2,1},{3,2},{4,3},{5,4},{6,5},{7,6},{8,7},{9,8},{10,9},{11,1... | collective-permute-start | bytes 49160 | tf_op jit(solution)/shard_map/ppermute | solution.py:26
  197.3 1.2 collective-permute-start.25
  232.4 3.2 %collective-permute-start.26 = (f32[1,4,1,1024]{3,2,1,0:T(1,128)S(1)}, f32[1,4,1,1024]{3,2,1,0:T(1,128)S(1)}, u32[]{:S(2)}, u32[]{:S(2)}) collective-permute-start(f32[1,4,1,1024]{3,2,1,0:T(1,128)S(1)} %get-tuple-element.58), channel_id=1, source_target_pairs={{1,0},{2,1},{3,2},{4,3},{5,4},{6,5},{7,6},{8,7},{9,8},{10,9},{11,1... | collective-permute-start | bytes 49160 | tf_op jit(solution)/shard_map/ppermute | solution.py:26
  233.1 2.5 collective-permute-start.27
  268.3 3.2 %collective-permute-start.28 = (f32[1,4,1,1024]{3,2,1,0:T(1,128)S(1)}, f32[1,4,1,1024]{3,2,1,0:T(1,128)S(1)}, u32[]{:S(2)}, u32[]{:S(2)}) collective-permute-start(f32[1,4,1,1024]{3,2,1,0:T(1,128)S(1)} %get-tuple-element.56), channel_id=1, source_target_pairs={{1,0},{2,1},{3,2},{4,3},{5,4},{6,5},{7,6},{8,7},{9,8},{10,9},{11,1... | collective-permute-start | bytes 49160 | tf_op jit(solution)/shard_map/ppermute | solution.py:26
  269.0 2.5 collective-permute-start.29
  304.2 1.4 collective-permute-start.30
  304.3 3.2 %collective-permute-start.31 = (f32[1,4,1,1024]{3,2,1,0:T(1,128)S(1)}, f32[1,4,1,1024]{3,2,1,0:T(1,128)S(1)}, u32[]{:S(2)}, u32[]{:S(2)}) collective-permute-start(f32[1,4,1,1024]{3,2,1,0:T(1,128)S(1)} %get-tuple-element.55), channel_id=1, source_target_pairs={{1,0},{2,1},{3,2},{4,3},{5,4},{6,5},{7,6},{8,7},{9,8},{10,9},{11,1... | collective-permute-start | bytes 49160 | tf_op jit(solution)/shard_map/ppermute | solution.py:26
where the time goes:
time: 312 us; the launch traced here: 308 us
  blocking collectives  196 us (63%)
  waiting for transfers between devices  58.7 us (19%)
  starting transfers between devices  42.6 us (14%)
  local copies, waits for them, and re-layouts  4.53 us (1%)
  other arithmetic  4.38 us (1%)
    psum x6, blocking collectives, paired_products(): lax.psum((local_sums(residual * residual), local_sums(residual * applied)...  196 us
    ppermute x8, waiting for transfers between devices, from_behind(): lax.ppermute(array, axis, [(i, (i + by) % length) for i in range(length)])  31.3 us
    ppermute x10, starting transfers between devices, extended(): lax.ppermute(head, axis, [((i + 1) % count, i) for i in range(count)])  22 us
    ppermute x12, starting transfers between devices, extended(): lax.ppermute(tail, axis, [(i, (i + 1) % count) for i in range(count)])  11.4 us
    ppermute x10, waiting for transfers between devices, extended(): lax.ppermute(head, axis, [((i + 1) % count, i) for i in range(count)])  11 us
    ppermute x12, waiting for transfers between devices, extended(): lax.ppermute(tail, axis, [(i, (i + 1) % count) for i in range(count)])  8.17 us
    ppermute x2, waiting for transfers between devices, passed_along(): return lax.ppermute(block, axis, route)  8.12 us
    ppermute x8, starting transfers between devices, from_behind(): lax.ppermute(array, axis, [(i, (i + by) % length) for i in range(length)])  6.63 us
  transfers between devices with their start and end apart: 32, of which 24 were waited for; matrix products, arithmetic and copies ran while one was open for 1% of the time, Pallas kernels for 0%

commit v1 on v0

v1 whole, which is shorter than its diff:
```python
import functools

import jax
import jax.numpy as jnp
from jax import lax
from jax.experimental import pallas as pl
from jax.experimental.pallas import tpu as pltpu
from jax.sharding import PartitionSpec as P

STEPS = 2

courant = 0.5
viscosity = 0.1
diagonal_add = 0.05
drag_rate = 2.0
block_cells = 64
centre = 4.0 + diagonal_add + 0.5 * drag_rate
MESH = pl.DeviceIdType.MESH


def radial_sum(x):
    cells = x.shape[1]
    lane = lax.broadcasted_iota(jnp.int32, x.shape, 1)
    before = jnp.where(lane == 0, 0.0, pltpu.roll(x, 1, 1))
    after = jnp.where(lane == cells - 1, 0.0, pltpu.roll(x, cells - 1, 1))
    return before + after


def step_kernel(
    n, pairs, ax, az, ra, drag, inflow, ax_out, az_out, ra_out, outlet_out,
    pred, wide, diag, tell_a, hear_a, tell_b, hear_b, sums,
    send_a, recv_a, send_b, recv_b, send_s, recv_s,
):
    layers, rows, cells = ax.shape
    me = lax.axis_index("az")
    sleeve = lax.axis_index("sec") == 1
    right, left = lax.rem(me + 1, n), lax.rem(me + n - 1, n)
    fields = (ax, az, ra)
    outs = (ax_out, az_out, ra_out)

    barrier = pltpu.get_barrier_semaphore()

    def greet(k, carry):
        pl.semaphore_signal(barrier, inc=1, device_id={"az": lax.rem(me + k, n)}, device_id_type=MESH)
        return carry

    lax.fori_loop(1, n, greet, 0)

    lane = lax.broadcasted_iota(jnp.int32, (rows, cells), 1)
    flags = drag[...].astype(jnp.float32)
    spread = jnp.zeros((rows, cells), jnp.float32)
    for block in range(drag.shape[1]):
        spread = jnp.where(lane // block_cells == block, flags[:, block : block + 1], spread)
    diag[...] = jnp.zeros_like(diag)
    diag[0:rows, :] = 4.0 + diagonal_add - centre + drag_rate * spread

    for f in range(3):
        for l in range(layers):
            at = f * layers + l
            tell_a[0, at : at + 1, :] = fields[f][l, 0:1, :]
            tell_a[1, at : at + 1, :] = fields[f][l, rows - 1 : rows, :]
    at = 3 * layers
    tell_a[0, at : at + 2, :] = diag[0:2, :]
    tell_a[1, at : at + 1, :] = diag[rows - 1 : rows, :]
    pl.semaphore_wait(barrier, n - 1)

    def exchange(tell, hear, send, recv):
        copies = []
        for slot, to in ((0, left), (1, right)):
            copy = pltpu.make_async_remote_copy(
                src_ref=tell.at[slot], dst_ref=hear.at[slot],
                send_sem=send.at[slot], recv_sem=recv.at[slot],
                device_id={"az": to}, device_id_type=MESH,
            )
            copy.start()
            copies.append(copy)
        return copies

    copies_a = exchange(tell_a, hear_a, send_a, recv_a)
    for copy in copies_a:
        copy.wait()
    diag[rows : rows + 2, :] = hear_a[0, at : at + 2, :]
    diag[2 * rows - 1 : 2 * rows, :] = hear_a[1, at : at + 1, :]

    row = lax.broadcasted_iota(jnp.int32, (rows, cells), 0)
    for f in range(3):
        own_outlet = fields[f][layers - 1]
        turned = jnp.concatenate([inflow[f, pl.ds(pairs[j], 1), :] for j in range(rows)], axis=0)
        upstream = jnp.where(sleeve, turned, own_outlet)
        for l in range(layers):
            x = fields[f][l]
            above = jnp.where(row == 0, hear_a[1, f * layers + l : f * layers + l + 1, :], pltpu.roll(x, 1, 0))
            below = jnp.where(
                row == rows - 1, hear_a[0, f * layers + l : f * layers + l + 1, :], pltpu.roll(x, rows - 1, 0)
            )
            around = above + below + radial_sum(x)
            pred[f, l] = x - courant * (x - upstream) + viscosity * (around - 4.0 * x)
            upstream = x

    for l in range(layers):
        v, w = pred[1, l], pred[2, l]
        v_prev = jnp.where(row == 0, 0.0, pltpu.roll(v, 1, 0))
        w_prev = jnp.where(lane == 0, 0.0, pltpu.roll(w, 1, 1))
        wide[l, 0:rows, :] = v - v_prev + (w - w_prev)
        tell_b[0, 4 * l : 4 * l + 3, :] = wide[l, 0:3, :]
        tell_b[1, 4 * l : 4 * l + 2, :] = wide[l, rows - 2 : rows, :]
        tell_b[1, 4 * l + 2 : 4 * l + 3, :] = v[rows - 1 : rows, :]
    copies_b = exchange(tell_b, hear_b, send_b, recv_b)
    for copy in copies_b:
        copy.wait()

    c_diag = diag[...]

    def apply(x):
        ring = 2 * rows
        return c_diag * x - (pltpu.roll(x, 1, 0) + pltpu.roll(x, ring - 1, 0) + radial_sum(x))

    def total(x):
        folded = x[:, 0:128]
        for c in range(1, cells // 128):
            folded = folded + x[:, c * 128 : (c + 1) * 128]
        return jnp.sum(folded, axis=0, keepdims=True)

    basis = []
    for l in range(layers):
        wide[l, 0:1, :] = wide[l, 0:1, :] - hear_b[1, 4 * l + 2 : 4 * l + 3, :]
        wide[l, rows : 2 * rows, :] = jnp.zeros((rows, cells), jnp.float32)
        wide[l, rows : rows + 1, :] = hear_b[0, 4 * l : 4 * l + 1, :] - pred[1, l, rows - 1 : rows, :]
        wide[l, rows + 1 : rows + 3, :] = hear_b[0, 4 * l + 1 : 4 * l + 3, :]
        wide[l, 2 * rows - 2 : 2 * rows, :] = hear_b[1, 4 * l : 4 * l + 2, :]
        b = wide[l]
        v1 = apply(b)
        v2 = apply(v1)
        b0, b1, b2 = b[0:rows], v1[0:rows], v2[0:rows]
        next_row = pltpu.roll(v2, 2 * rows - 1, 0)[0:rows]
        next_cell = jnp.where(lane == cells - 1, 0.0, pltpu.roll(b2, cells - 1, 1))
        parts = (b0 * b0, b0 * b1, b1 * b1, b1 * b2, b2 * b2, b2 * (c_diag[0:rows] * b2 - 2.0 * (next_row + next_cell)))
        for k, part in enumerate(parts):
            sums[me, k, l : l + 1, :] = total(part)
        basis.append((v1, v2))

    def sum_copy(k, slot_of):
        return pltpu.make_async_remote_copy(
            src_ref=sums.at[me], dst_ref=sums.at[slot_of],
            send_sem=send_s.at[k], recv_sem=recv_s.at[slot_of],
            device_id={"az": lax.rem(me + k, n)}, device_id_type=MESH,
        )

    def give(k, carry):
        sum_copy(k, me).start()
        return carry

    def take(k, carry):
        sum_copy(k, me).wait_send()
        sum_copy(k, lax.rem(me + n - k, n)).wait_recv()
        return carry

    lax.fori_loop(1, n, give, 0)
    lax.fori_loop(1, n, take, 0)

    moments = lax.fori_loop(1, n, lambda j, acc: acc + sums[j], sums[0])
    m = [jnp.sum(moments[k], axis=1, keepdims=True) for k in range(6)]
    g = [m[k + 1] + centre * m[k] for k in range(5)]
    inv0 = 1.0 / g[0]
    l10, l20 = g[1] * inv0, g[2] * inv0
    d1 = g[2] - l10 * g[1]
    inv1 = jnp.where(d1 > 1e-7 * g[2], 1.0 / d1, 0.0)
    t21 = g[3] - l20 * g[1]
    l21 = t21 * inv1
    d2 = g[4] - l20 * g[2] - l21 * t21
    inv2 = jnp.where(d2 > 1e-7 * g[4], 1.0 / d2, 0.0)
    y0 = m[0]
    y1 = m[1] - l10 * y0
    y2 = m[2] - l20 * y0 - l21 * y1
    c2 = y2 * inv2
    c1 = y1 * inv1 - l21 * c2
    c0 = y0 * inv0 - l10 * c1 - l20 * c2

    for l in range(layers):
        v1, v2 = basis[l]
        pressure = c0[l : l + 1] * wide[l] + c1[l : l + 1] * v1 + c2[l : l + 1] * v2
        p = pressure[0:rows]
        p_row = pltpu.roll(pressure, 2 * rows - 1, 0)[0:rows]
        p_cell = jnp.where(lane == cells - 1, 0.0, pltpu.roll(p, cells - 1, 1))
        results = (pred[0, l], pred[1, l] - (p_row - p), pred[2, l] - (p_cell - p))
        for f in range(3):
            outs[f][l] = results[f]
            if l == layers - 1:
                outlet_out[f] = results[f]


def step(n, pairs, ax, az, ra, drag, inflow):
    layers, rows, cells = ax.shape
    f32 = jnp.float32
    vmem = pl.BlockSpec(memory_space=pltpu.VMEM)
    field = jax.ShapeDtypeStruct(ax.shape, f32)
    told = -(-(3 * layers + 2) // 8) * 8
    return pl.pallas_call(
        functools.partial(step_kernel, n),
        out_shape=(field, field, field, jax.ShapeDtypeStruct((3, rows, cells), f32)),
        in_specs=[pl.BlockSpec(memory_space=pltpu.SMEM)] + [vmem] * 5,
        out_specs=(vmem,) * 4,
        scratch_shapes=[
            pltpu.VMEM((3, layers, rows, cells), f32),
            pltpu.VMEM((layers, 2 * rows, cells), f32),
            pltpu.VMEM((2 * rows, cells), f32),
            pltpu.VMEM((2, told, cells), f32),
            pltpu.VMEM((2, told, cells), f32),
            pltpu.VMEM((2, 4 * layers, cells), f32),
            pltpu.VMEM((2, 4 * layers, cells), f32),
            pltpu.VMEM((n, 6, layers, 128), f32),
            pltpu.SemaphoreType.DMA((2,)),
            pltpu.SemaphoreType.DMA((2,)),
            pltpu.SemaphoreType.DMA((2,)),
            pltpu.SemaphoreType.DMA((2,)),
            pltpu.SemaphoreType.DMA((n,)),
            pltpu.SemaphoreType.DMA((n,)),
        ],
        compiler_params=pltpu.CompilerParams(
            collective_id=0, has_side_effects=True, vmem_limit_bytes=24 * 1024 * 1024
        ),
    )(pairs, ax, az, ra, drag, inflow)


def turned_inflow(outlet, turn, n):
    def route(shift):
        pairs = [(b, n + (b + shift) % n) for b in range(n)]
        return lambda plane: lax.ppermute(plane, ("sec", "az"), pairs)

    return lax.switch(turn, [route(shift) for shift in range(n)], outlet)


def body(axial, azimuthal, radial, drag_blocks, rotation, row_pairs):
    n = lax.axis_size("az")
    ax, az, ra, drag = axial[0], azimuthal[0], radial[0], drag_blocks[0]
    outlet = jnp.stack([ax[-1], az[-1], ra[-1]])
    for time_step in range(STEPS):
        inflow = turned_inflow(outlet, rotation[0] * (time_step + 1) % n, n)
        ax, az, ra, outlet = step(n, row_pairs, ax, az, ra, drag, inflow)
    return ax[None], az[None], ra[None]


def solution(mesh):
    field = P("sec", None, "az", None)
    return jax.shard_map(
        body,
        mesh=mesh,
        in_specs=(field, field, field, P("sec", "az", None), P(), P()),
        out_specs=(field, field, field),
        check_vma=False,
    )
```

time: 312 us -> 64.9 us (0.21)
  blocking collectives: 196 us -> 0 us
  waiting for transfers between devices: 58.7 us -> 11 us
  Pallas kernels: 0 us -> 44.4 us
  starting transfers between devices: 42.6 us -> 2.72 us
  other arithmetic: 4.38 us -> 0.01 us
    psum x6 -> x0, blocking collectives: 196 us -> none  [paired_products(): lax.psum((local_sums(residual * residual), local_sums(residual * applied)...]
    ppermute x32 -> x2, waiting for transfers between devices: 58.7 us -> 11 us  [route(): return lambda plane: lax.ppermute(plane, ('sec', 'az'), pairs)]
    pallas_call x0 -> x2, Pallas kernels: none -> 44.4 us  [step(): pl.pallas_call(functools.partial(step_kernel, n), out_shape=(field, field...]
    ppermute x32 -> x2, starting transfers between devices: 42.6 us -> 2.72 us  [route(): return lambda plane: lax.ppermute(plane, ('sec', 'az'), pairs)]
  transfers between devices with their start and end apart: 32 -> 2, of which waited for: 24 -> 2; matrix products, arithmetic and copies ran while one was open for 1% -> 0% of each run, Pallas kernels for 0% -> 0%
where the time goes in v1:
time: 64.9 us; the launch traced here: 63.9 us
  Pallas kernels  44.4 us (68%)
  waiting for transfers between devices  11 us (17%)
  local copies, waits for them, and re-layouts  4.22 us (7%)
  starting transfers between devices  2.72 us (4%)
  between operations  1.4 us (2%)
    pallas_call x2, Pallas kernels, step(): pl.pallas_call(functools.partial(step_kernel, n), out_shape=(field, field...  44.4 us
    ppermute x2, waiting for transfers between devices, route(): return lambda plane: lax.ppermute(plane, ('sec', 'az'), pairs)  11 us
    ppermute x2, starting transfers between devices, route(): return lambda plane: lax.ppermute(plane, ('sec', 'az'), pairs)  2.72 us
    unnamed x13, local copies, waits for them, and re-layouts  2.62 us
    slice x2, local copies, waits for them, and re-layouts, body(): outlet = jnp.stack([ax[-1], az[-1], ra[-1]])  1.6 us
  transfers between devices with their start and end apart: 2, of which 2 were waited for; matrix products, arithmetic and copies ran while one was open for 0% of the time, Pallas kernels for 0%

profile of v1, /device:TPU:3, one launch (start us, length us, event | category | flops | bytes accessed | tf_op | source)
XLA Modules:
  0.0 63.9 jit_solution(11308606820634549749)
XLA Ops:
  0.6 0.0 copy-start.1
  1.4 0.8 %slice_bitcast_fusion.2 = f32[1,8,1024]{2,1,0:T(8,128)S(1)} fusion(f32[1,4,8,1024]{3,2,1,0:T(8,128)} %param.38), kind=kLoop, calls=%fused_computation.3 | loop fusion | bytes 65536 | tf_op jit(solution)/shard_map/slice | solution.py:236
  2.1 0.0 copy-done.1
  2.1 0.0 copy-start.2
  2.1 0.8 %slice_bitcast_fusion = (f32[1,8,1024]{2,1,0:T(8,128)S(1)}, f32[1,8,1024]{2,1,0:T(8,128)S(1)}) fusion(f32[1,4,8,1024]{3,2,1,0:T(8,128)} %param.40, f32[1,4,8,1024]{3,2,1,0:T(8,128)S(1)} %copy-done.1), kind=kLoop, calls=%fused_computation.1 | loop fusion | bytes 131072 | tf_op jit(solution)/shard_map/slice | solution.py:236
  3.0 0.0 copy-start
  3.0 0.0 copy-start.3
  3.0 6.5 %conditional.2 = (f32[3,8,1024]{2,1,0:T(8,128)}) conditional(s32[]{:T(128)} %clamp.6, f32[3,8,1024]{2,1,0:T(8,128)S(1)} %pad_maximum_fusion, f32[3,8,1024]{2,1,0:T(8,128)S(1)} %pad_maximum_fusion, f32[3,8,1024]{2,1,0:T(8,128)S(1)} %pad_maximum_fusion, f32[3,8,1024]{2,1,0:T(8,128)S(1)} %pad_maximum_fusion, ...), branch_computations={%region_0.1_spmd, %region_1.2_spmd, %region_2.3_spmd, %region_3.4_... | conditional | bytes 393264 | solution.py:230
  3.0 1.4 %collective-permute-start.12 = (f32[3,8,1024]{2,1,0:T(8,128)S(1)}, f32[3,8,1024]{2,1,0:T(8,128)}, u32[]{:S(2)}, u32[]{:S(2)}) collective-permute-start(f32[3,8,1024]{2,1,0:T(8,128)S(1)} %param.12), channel_id=1, source_target_pairs={{0,28},{1,29},{2,30},{3,31},{4,16},{5,17},{6,18},{7,19},{8,20},{9,... | collective-permute-start | bytes 294920 | tf_op jit(solution)/shard_map/cond/branch_12_fun/ppermute | solution.py:228
  4.4 5.1 %collective-permute-done.12 = f32[3,8,1024]{2,1,0:T(8,128)} collective-permute-done((f32[3,8,1024]{2,1,0:T(8,128)S(1)}, f32[3,8,1024]{2,1,0:T(8,128)}, u32[]{:S(2)}, u32[]{:S(2)}) %collective-permute-start.12) | collective-permute-done | bytes 98336 | tf_op jit(solution)/shard_map/cond/branch_12_fun/ppermute | solution.py:228
  9.5 0.0 copy-start.4
  9.5 0.0 copy-done.2
  9.5 0.0 copy-done
  9.5 0.0 copy-done.3
  9.5 0.6 copy-done.4
  10.2 21.2 %shard_map.85 = (f32[4,8,1024]{2,1,0:T(8,128)S(1)}, f32[4,8,1024]{2,1,0:T(8,128)S(1)}, f32[4,8,1024]{2,1,0:T(8,128)S(1)}, f32[3,8,1024]{2,1,0:T(8,128)S(1)}) custom-call(s32[8]{0:T(128)S(1)} %copy-done.4, f32[4,8,1024]{2,1,0:T(8,128)S(1)} %bitcast.18, f32[4,8,1024]{2,1,0:T(8,128)S(1)} %bitcast.19, f32[4,8,1024]{2,1,0:T(8,128)S(1)} %bitcast.20, ...), custom_call_target="tpu_custom_call" | custom-call | tf_op jit(solution)/shard_map/pallas_call | solution.py:198
  31.4 7.3 %conditional.3 = (f32[3,8,1024]{2,1,0:T(8,128)}) conditional(s32[]{:T(128)} %clamp.7, f32[3,8,1024]{2,1,0:T(8,128)S(1)} %get-tuple-element.79, f32[3,8,1024]{2,1,0:T(8,128)S(1)} %get-tuple-element.79, f32[3,8,1024]{2,1,0:T(8,128)S(1)} %get-tuple-element.79, f32[3,8,1024]{2,1,0:T(8,128)S(1)} %get-tuple-element.79, ...), branch_computations={%region_16.17_spmd, %region_17.18_spmd, %region_18.19_spmd, %regio... | conditional | bytes 393264 | solution.py:230
  31.4 1.3 %collective-permute-start.24 = (f32[3,8,1024]{2,1,0:T(8,128)S(1)}, f32[3,8,1024]{2,1,0:T(8,128)}, u32[]{:S(2)}, u32[]{:S(2)}) collective-permute-start(f32[3,8,1024]{2,1,0:T(8,128)S(1)} %param.24), channel_id=1, source_target_pairs={{0,24},{1,25},{2,26},{3,27},{4,28},{5,29},{6,30},{7,31},{8,16},{9,... | collective-permute-start | bytes 294920 | tf_op jit(solution)/shard_map/cond/branch_8_fun/ppermute | solution.py:228
  32.7 6.0 %collective-permute-done.24 = f32[3,8,1024]{2,1,0:T(8,128)} collective-permute-done((f32[3,8,1024]{2,1,0:T(8,128)S(1)}, f32[3,8,1024]{2,1,0:T(8,128)}, u32[]{:S(2)}, u32[]{:S(2)}) %collective-permute-start.24) | collective-permute-done | bytes 98336 | tf_op jit(solution)/shard_map/cond/branch_8_fun/ppermute | solution.py:228
  38.7 23.2 %shard_map.86 = (f32[4,8,1024]{2,1,0:T(8,128)S(1)}, f32[4,8,1024]{2,1,0:T(8,128)S(1)}, f32[4,8,1024]{2,1,0:T(8,128)S(1)}, f32[3,8,1024]{2,1,0:T(8,128)}) custom-call(s32[8]{0:T(128)S(1)} %copy-done.4, f32[4,8,1024]{2,1,0:T(8,128)S(1)} %get-tuple-element.76.ax, f32[4,8,1024]{2,1,0:T(8,128)S(1)} %get-tuple-element.77.az, ...), custom_call_target="tpu_custom_call" | custom-call | tf_op jit(solution)/shard_map/pallas_call | solution.py:198
  61.9 0.7 %copy.45 = f32[1,4,8,1024]{3,2,1,0:T(8,128)} copy(f32[1,4,8,1024]{3,2,1,0:T(8,128)S(1)} %bitcast.23) | data formatting | bytes 262144
  62.6 0.7 %copy.46 = f32[1,4,8,1024]{3,2,1,0:T(8,128)} copy(f32[1,4,8,1024]{3,2,1,0:T(8,128)S(1)} %bitcast.22) | data formatting | bytes 262144
  63.2 0.7 %copy.47 = f32[1,4,8,1024]{3,2,1,0:T(8,128)} copy(f32[1,4,8,1024]{3,2,1,0:T(8,128)S(1)} %bitcast.21) | data formatting | bytes 262144
  (1 shorter events, 0.0 us)
Async XLA Ops:
  0.6 1.5 %copy-start.1 = (f32[1,4,8,1024]{3,2,1,0:T(8,128)S(1)}, f32[1,4,8,1024]{3,2,1,0:T(8,128)}, u32[]{:S(2)}) copy-start(f32[1,4,8,1024]{3,2,1,0:T(8,128)} %param.39) | copy-start | bytes 393220
  2.1 7.4 %copy-start.2 = (f32[1,4,8,1024]{3,2,1,0:T(8,128)S(1)}, f32[1,4,8,1024]{3,2,1,0:T(8,128)}, u32[]{:S(2)}) copy-start(f32[1,4,8,1024]{3,2,1,0:T(8,128)} %param.40) | copy-start | bytes 393220
  3.0 6.6 %copy-start = (f32[1,4,8,1024]{3,2,1,0:T(8,128)S(1)}, f32[1,4,8,1024]{3,2,1,0:T(8,128)}, u32[]{:S(2)}) copy-start(f32[1,4,8,1024]{3,2,1,0:T(8,128)} %param.38) | copy-start | bytes 393220
  3.0 6.6 %copy-start.3 = (s32[1,8,16]{2,1,0:T(8,128)S(1)}, s32[1,8,16]{2,1,0:T(8,128)}, u32[]{:S(2)}) copy-start(s32[1,8,16]{2,1,0:T(8,128)} %param.41) | copy-start | bytes 1540
  3.0 6.5 %collective-permute-start.12 = (f32[3,8,1024]{2,1,0:T(8,128)S(1)}, f32[3,8,1024]{2,1,0:T(8,128)}, u32[]{:S(2)}, u32[]{:S(2)}) collective-permute-start(f32[3,8,1024]{2,1,0:T(8,128)S(1)} %param.12), channel_id=1, source_target_pairs={{0,28},{1,29},{2,30},{3,31},{4,16},{5,17},{6,18},{7,19},{8,20},{9,... | collective-permute-start | bytes 294920 | tf_op jit(solution)/shard_map/cond/branch_12_fun/ppermute | solution.py:228
  9.5 0.7 %copy-start.4 = (s32[8]{0:T(128)S(1)}, s32[8]{0:T(128)}, u32[]{:S(2)}) copy-start(s32[8]{0:T(128)} %pairs.3) | copy-start | bytes 100
  31.4 7.3 %collective-permute-start.24 = (f32[3,8,1024]{2,1,0:T(8,128)S(1)}, f32[3,8,1024]{2,1,0:T(8,128)}, u32[]{:S(2)}, u32[]{:S(2)}) collective-permute-start(f32[3,8,1024]{2,1,0:T(8,128)S(1)} %param.24), channel_id=1, source_target_pairs={{0,24},{1,25},{2,26},{3,27},{4,28},{5,29},{6,30},{7,31},{8,16},{9,... | collective-permute-start | bytes 294920 | tf_op jit(solution)/shard_map/cond/branch_8_fun/ppermute | solution.py:228

commit v2 on v1

v2 whole, which is shorter than its diff:
```python
import functools

import jax
import jax.numpy as jnp
from jax import lax
from jax.experimental import pallas as pl
from jax.experimental.pallas import tpu as pltpu
from jax.sharding import PartitionSpec as P

STEPS = 2

courant = 0.5
viscosity = 0.1
diagonal_add = 0.05
drag_rate = 2.0
block_cells = 64
centre = 4.0 + diagonal_add + 0.5 * drag_rate
MESH = pl.DeviceIdType.MESH


def radial_sum(x):
    cells = x.shape[1]
    lane = lax.broadcasted_iota(jnp.int32, x.shape, 1)
    before = jnp.where(lane == 0, 0.0, pltpu.roll(x, 1, 1))
    after = jnp.where(lane == cells - 1, 0.0, pltpu.roll(x, cells - 1, 1))
    return before + after


def steps_kernel(
    n, pairs, rotation, ax, az, ra, drag, ax_out, az_out, ra_out,
    mid, pred, wide, diag, tell_a, hear_a, tell_b, hear_b, sums, plane, got, inflow, landing,
    send_a, recv_a, send_b, recv_b, send_s, recv_s, send_p, recv_p, send_x, recv_x,
):
    layers, rows, cells = ax.shape
    stages = got.shape[0]
    me = lax.axis_index("az")
    sleeve = lax.axis_index("sec") == 1
    precursor = lax.axis_index("sec") == 0
    right, left = lax.rem(me + 1, n), lax.rem(me + n - 1, n)

    barrier = pltpu.get_barrier_semaphore()

    def greet(k, carry):
        pl.semaphore_signal(barrier, inc=1, device_id={"az": lax.rem(me + k, n)}, device_id_type=MESH)
        return carry

    lax.fori_loop(1, n, greet, 0)
    pl.semaphore_signal(
        barrier, inc=1, device_id={"sec": 1 - lax.axis_index("sec")}, device_id_type=MESH
    )

    lane = lax.broadcasted_iota(jnp.int32, (rows, cells), 1)
    row = lax.broadcasted_iota(jnp.int32, (rows, cells), 0)
    flags = drag[...].astype(jnp.float32)
    spread = jnp.zeros((rows, cells), jnp.float32)
    for block in range(drag.shape[1]):
        spread = jnp.where(lane // block_cells == block, flags[:, block : block + 1], spread)
    diag[...] = jnp.zeros_like(diag)
    diag[0:rows, :] = 4.0 + diagonal_add - centre + drag_rate * spread

    def exchange(tell, hear, send, recv):
        copies = []
        for slot, to in ((0, left), (1, right)):
            copy = pltpu.make_async_remote_copy(
                src_ref=tell.at[slot], dst_ref=hear.at[slot],
                send_sem=send.at[slot], recv_sem=recv.at[slot],
                device_id={"az": to}, device_id_type=MESH,
            )
            copy.start()
            copies.append(copy)
        return copies

    def cross(which, f, src, dst):
        return pltpu.make_async_remote_copy(
            src_ref=src, dst_ref=dst, send_sem=send_x.at[which, f], recv_sem=recv_x.at[which, f],
            device_id={"sec": 1}, device_id_type=MESH,
        )

    def stage_copy(k, f):
        return pltpu.make_async_remote_copy(
            src_ref=plane.at[k, f], dst_ref=got.at[k, f],
            send_sem=send_p.at[k, f], recv_sem=recv_p.at[k, f],
            device_id={"az": lax.rem(me + (1 << k) % n, n)}, device_id_type=MESH,
        )

    def turn_plane(turn, ready=None):
        for f in range(3):
            if ready is not None:
                ready(f)
            stage_copy(0, f).start()
        for k in range(stages):
            moves = lax.rem(lax.div(turn, 1 << k), 2) == 1
            for f in range(3):
                stage_copy(k, f).wait_recv()
                plane[k + 1, f] = jnp.where(moves, got[k, f], plane[k, f])
                if k + 1 < stages:
                    stage_copy(k + 1, f).start()

    def turn_sent():
        for k in range(stages):
            for f in range(3):
                stage_copy(k, f).wait_send()

    c_rows = 3 * layers
    for time_step in range(STEPS):
        first, last = time_step == 0, time_step == STEPS - 1
        fields = (ax, az, ra) if first else tuple(mid.at[f] for f in range(3))
        outs = (ax_out, az_out, ra_out) if last else tuple(mid.at[f] for f in range(3))
        turn = lax.rem(rotation[0] * (time_step + 1), n)
        ta, ha = tell_a.at[time_step], hear_a.at[time_step]
        tb, hb = tell_b.at[time_step], hear_b.at[time_step]
        ss = sums.at[time_step]

        for f in range(3):
            for l in range(layers):
                at = f * layers + l
                ta[0, at : at + 1, :] = fields[f][l, 0:1, :]
                ta[1, at : at + 1, :] = fields[f][l, rows - 1 : rows, :]
        if first:
            ta[0, c_rows : c_rows + 2, :] = diag[0:2, :]
            ta[1, c_rows : c_rows + 1, :] = diag[rows - 1 : rows, :]
            pl.semaphore_wait(barrier, n)

            @pl.when(precursor)
            def _():
                for f in range(3):
                    cross(0, f, (ax, az, ra)[f].at[layers - 1], plane.at[0, f]).start()

        copies_a = exchange(ta, ha, send_a.at[time_step], recv_a.at[time_step])
        if first:
            @pl.when(sleeve)
            def _():
                turn_plane(turn, lambda f: cross(0, f, plane.at[0, f], plane.at[0, f]).wait_recv())
        else:
            @pl.when(precursor)
            def _():
                for f in range(3):
                    plane[0, f] = fields[f][layers - 1]
                turn_plane(turn)
                for f in range(3):
                    cross(1, f, plane.at[stages, f], landing.at[f]).start()
                turn_sent()

        for copy in copies_a:
            copy.wait()
        if first:
            diag[rows : rows + 2, :] = ha[0, c_rows : c_rows + 2, :]
            diag[2 * rows - 1 : 2 * rows, :] = ha[1, c_rows : c_rows + 1, :]

            @pl.when(sleeve)
            def _():
                for f in range(3):
                    inflow[f] = plane[stages, f]
                turn_sent()

            @pl.when(precursor)
            def _():
                for f in range(3):
                    cross(0, f, (ax, az, ra)[f].at[layers - 1], plane.at[0, f]).wait_send()
                    inflow[f] = (ax, az, ra)[f][layers - 1]
        else:
            @pl.when(sleeve)
            def _():
                for f in range(3):
                    cross(1, f, plane.at[stages, f], landing.at[f]).wait_recv()
                    inflow[f] = landing[f]

        for f in range(3):
            turned = jnp.concatenate([inflow[f, pl.ds(pairs[j], 1), :] for j in range(rows)], axis=0)
            upstream = jnp.where(sleeve, turned, fields[f][layers - 1])
            for l in range(layers):
                x = fields[f][l]
                at = f * layers + l
                above = jnp.where(row == 0, ha[1, at : at + 1, :], pltpu.roll(x, 1, 0))
                below = jnp.where(row == rows - 1, ha[0, at : at + 1, :], pltpu.roll(x, rows - 1, 0))
                around = above + below + radial_sum(x)
                pred[f, l] = x - courant * (x - upstream) + viscosity * (around - 4.0 * x)
                upstream = x

        for l in range(layers):
            v, w = pred[1, l], pred[2, l]
            v_prev = jnp.where(row == 0, 0.0, pltpu.roll(v, 1, 0))
            w_prev = jnp.where(lane == 0, 0.0, pltpu.roll(w, 1, 1))
            wide[l, 0:rows, :] = v - v_prev + (w - w_prev)
            tb[0, 4 * l : 4 * l + 3, :] = wide[l, 0:3, :]
            tb[1, 4 * l : 4 * l + 2, :] = wide[l, rows - 2 : rows, :]
            tb[1, 4 * l + 2 : 4 * l + 3, :] = v[rows - 1 : rows, :]
        for copy in exchange(tb, hb, send_b.at[time_step], recv_b.at[time_step]):
            copy.wait()

        c_diag = diag[...]

        def apply(x):
            ring = 2 * rows
            return c_diag * x - (pltpu.roll(x, 1, 0) + pltpu.roll(x, ring - 1, 0) + radial_sum(x))

        def total(x):
            folded = x[:, 0:128]
            for c in range(1, cells // 128):
                folded = folded + x[:, c * 128 : (c + 1) * 128]
            return jnp.sum(folded, axis=0, keepdims=True)

        basis = []
        for l in range(layers):
            wide[l, 0:1, :] = wide[l, 0:1, :] - hb[1, 4 * l + 2 : 4 * l + 3, :]
            wide[l, rows : 2 * rows, :] = jnp.zeros((rows, cells), jnp.float32)
            wide[l, rows : rows + 1, :] = hb[0, 4 * l : 4 * l + 1, :] - pred[1, l, rows - 1 : rows, :]
            wide[l, rows + 1 : rows + 3, :] = hb[0, 4 * l + 1 : 4 * l + 3, :]
            wide[l, 2 * rows - 2 : 2 * rows, :] = hb[1, 4 * l : 4 * l + 2, :]
            b = wide[l]
            v1 = apply(b)
            v2 = apply(v1)
            b0, b1, b2 = b[0:rows], v1[0:rows], v2[0:rows]
            next_row = pltpu.roll(v2, 2 * rows - 1, 0)[0:rows]
            next_cell = jnp.where(lane == cells - 1, 0.0, pltpu.roll(b2, cells - 1, 1))
            c_b2 = c_diag[0:rows] * b2 - 2.0 * (next_row + next_cell)
            parts = (b0 * b0, b0 * b1, b1 * b1, b1 * b2, b2 * b2, b2 * c_b2)
            for k, part in enumerate(parts):
                ss[me, k, l : l + 1, :] = total(part)
            basis.append((v1, v2))

        def sum_copy(k, slot_of):
            return pltpu.make_async_remote_copy(
                src_ref=ss.at[me], dst_ref=ss.at[slot_of],
                send_sem=send_s.at[time_step, k], recv_sem=recv_s.at[time_step, slot_of],
                device_id={"az": lax.rem(me + k, n)}, device_id_type=MESH,
            )

        def give(k, carry):
            sum_copy(k, me).start()
            return carry

        def take(k, carry):
            sum_copy(k, me).wait_send()
            sum_copy(k, lax.rem(me + n - k, n)).wait_recv()
            return carry

        lax.fori_loop(1, n, give, 0)
        lax.fori_loop(1, n, take, 0)

        moments = lax.fori_loop(1, n, lambda j, acc: acc + ss[j], ss[0])
        m = [jnp.sum(moments[k], axis=1, keepdims=True) for k in range(6)]
        g = [m[k + 1] + centre * m[k] for k in range(5)]
        inv0 = 1.0 / g[0]
        l10, l20 = g[1] * inv0, g[2] * inv0
        d1 = g[2] - l10 * g[1]
        inv1 = jnp.where(d1 > 1e-7 * g[2], 1.0 / d1, 0.0)
        t21 = g[3] - l20 * g[1]
        l21 = t21 * inv1
        d2 = g[4] - l20 * g[2] - l21 * t21
        inv2 = jnp.where(d2 > 1e-7 * g[4], 1.0 / d2, 0.0)
        y0 = m[0]
        y1 = m[1] - l10 * y0
        y2 = m[2] - l20 * y0 - l21 * y1
        c2 = y2 * inv2
        c1 = y1 * inv1 - l21 * c2
        c0 = y0 * inv0 - l10 * c1 - l20 * c2

        for l in range(layers):
            v1, v2 = basis[l]
            pressure = c0[l : l + 1] * wide[l] + c1[l : l + 1] * v1 + c2[l : l + 1] * v2
            p = pressure[0:rows]
            p_row = pltpu.roll(pressure, 2 * rows - 1, 0)[0:rows]
            p_cell = jnp.where(lane == cells - 1, 0.0, pltpu.roll(p, cells - 1, 1))
            outs[0][l] = pred[0, l]
            outs[1][l] = pred[1, l] - (p_row - p)
            outs[2][l] = pred[2, l] - (p_cell - p)

    @pl.when(precursor)
    def _():
        for f in range(3):
            cross(1, f, plane.at[stages, f], landing.at[f]).wait_send()


def steps(n, pairs, rotation, ax, az, ra, drag):
    layers, rows, cells = ax.shape
    f32 = jnp.float32
    stages = (n - 1).bit_length()
    vmem, smem = pl.BlockSpec(memory_space=pltpu.VMEM), pl.BlockSpec(memory_space=pltpu.SMEM)
    field = jax.ShapeDtypeStruct(ax.shape, f32)
    told = -(-(3 * layers + 2) // 8) * 8
    dma = pltpu.SemaphoreType.DMA
    return pl.pallas_call(
        functools.partial(steps_kernel, n),
        out_shape=(field, field, field),
        in_specs=[smem, smem] + [vmem] * 4,
        out_specs=(vmem,) * 3,
        scratch_shapes=[
            pltpu.VMEM((3, layers, rows, cells), f32),
            pltpu.VMEM((3, layers, rows, cells), f32),
            pltpu.VMEM((layers, 2 * rows, cells), f32),
            pltpu.VMEM((2 * rows, cells), f32),
            pltpu.VMEM((STEPS, 2, told, cells), f32),
            pltpu.VMEM((STEPS, 2, told, cells), f32),
            pltpu.VMEM((STEPS, 2, 4 * layers, cells), f32),
            pltpu.VMEM((STEPS, 2, 4 * layers, cells), f32),
            pltpu.VMEM((STEPS, n, 6, layers, 128), f32),
            pltpu.VMEM((stages + 1, 3, rows, cells), f32),
            pltpu.VMEM((stages, 3, rows, cells), f32),
            pltpu.VMEM((3, rows, cells), f32),
            pltpu.VMEM((3, rows, cells), f32),
            dma((STEPS, 2)),
            dma((STEPS, 2)),
            dma((STEPS, 2)),
            dma((STEPS, 2)),
            dma((STEPS, n)),
            dma((STEPS, n)),
            dma((stages, 3)),
            dma((stages, 3)),
            dma((2, 3)),
            dma((2, 3)),
        ],
        compiler_params=pltpu.CompilerParams(
            collective_id=0, has_side_effects=True, vmem_limit_bytes=32 * 1024 * 1024
        ),
    )(pairs, rotation, ax, az, ra, drag)


def body(axial, azimuthal, radial, drag_blocks, rotation, row_pairs):
    n = lax.axis_size("az")
    outs = steps(n, row_pairs, rotation, axial[0], azimuthal[0], radial[0], drag_blocks[0])
    return tuple(out[None] for out in outs)


def solution(mesh):
    field = P("sec", None, "az", None)
    return jax.shard_map(
        body,
        mesh=mesh,
        in_specs=(field, field, field, P("sec", "az", None), P(), P()),
        out_specs=(field, field, field),
        check_vma=False,
    )
```

time: 64.9 us -> 56.4 us (0.87); the launches traced: 63.9 us -> 56.2 us
  waiting for transfers between devices: 11 us -> 0 us
  Pallas kernels: 44.4 us -> 49.5 us
  starting transfers between devices: 2.72 us -> 0 us
  local copies, waits for them, and re-layouts: 4.22 us -> 5.35 us
    ppermute x2 -> x0, waiting for transfers between devices: 11 us -> none  [route(): return lambda plane: lax.ppermute(plane, ('sec', 'az'), pairs)]
    pallas_call x2 -> x1, Pallas kernels: 44.4 us -> 49.5 us  [steps(): pl.pallas_call(functools.partial(steps_kernel, n), out_shape=(field, fiel...]
    unnamed x13, local copies, waits for them, and re-layouts: 2.62 us -> 5.35 us
    ppermute x2 -> x0, starting transfers between devices: 2.72 us -> none  [route(): return lambda plane: lax.ppermute(plane, ('sec', 'az'), pairs)]
    slice x2 -> x0, local copies, waits for them, and re-layouts: 1.6 us -> none  [body(): outlet = jnp.stack([ax[-1], az[-1], ra[-1]])]
  transfers between devices with their start and end apart: 2 -> 0, of which waited for: 2 -> 0; matrix products, arithmetic and copies ran while one was open for 0% -> 0% of each run, Pallas kernels for 0% -> 0%
where the time goes in v2:
time: 56.4 us; the launch traced here: 56.2 us
  Pallas kernels  49.5 us (88%)
  local copies, waits for them, and re-layouts  5.35 us (9%)
  between operations  1.31 us (2%)
    pallas_call x1, Pallas kernels, steps(): pl.pallas_call(functools.partial(steps_kernel, n), out_shape=(field, fiel...  49.5 us
    unnamed x13, local copies, waits for them, and re-layouts  5.35 us

profile of v2, /device:TPU:3, one launch (start us, length us, event | category | flops | bytes accessed | tf_op | source)
XLA Modules:
  0.0 56.2 jit_solution(9434058513319076985)
XLA Ops:
  1.3 0.0 copy-start.3
  1.3 0.0 copy-start.4
  1.3 0.7 %copy-done.3 = s32[1,8,16]{2,1,0:T(8,128)S(1)} copy-done((s32[1,8,16]{2,1,0:T(8,128)S(1)}, s32[1,8,16]{2,1,0:T(8,128)}, u32[]{:S(2)}) %copy-start.3) | copy-done | bytes 536
  2.0 0.0 copy-done.4
  2.0 0.0 copy-start
  2.0 0.9 %copy-done = f32[1,4,8,1024]{3,2,1,0:T(8,128)S(1)} copy-done((f32[1,4,8,1024]{3,2,1,0:T(8,128)S(1)}, f32[1,4,8,1024]{3,2,1,0:T(8,128)}, u32[]{:S(2)}) %copy-start) | copy-done | bytes 131096
  2.9 0.0 copy-start.1
  2.9 0.9 %copy-done.1 = f32[1,4,8,1024]{3,2,1,0:T(8,128)S(1)} copy-done((f32[1,4,8,1024]{3,2,1,0:T(8,128)S(1)}, f32[1,4,8,1024]{3,2,1,0:T(8,128)}, u32[]{:S(2)}) %copy-start.1) | copy-done | bytes 131096
  3.8 0.0 copy-start.2
  3.8 0.9 %copy-done.2 = f32[1,4,8,1024]{3,2,1,0:T(8,128)S(1)} copy-done((f32[1,4,8,1024]{3,2,1,0:T(8,128)S(1)}, f32[1,4,8,1024]{3,2,1,0:T(8,128)}, u32[]{:S(2)}) %copy-start.2) | copy-done | bytes 131096
  4.7 49.5 %shard_map.85 = (f32[4,8,1024]{2,1,0:T(8,128)S(1)}, f32[4,8,1024]{2,1,0:T(8,128)S(1)}, f32[4,8,1024]{2,1,0:T(8,128)S(1)}) custom-call(s32[8]{0:T(128)S(1)} %copy-done.4, s32[1]{0:T(128)S(6)} %copy.12.rotation, f32[4,8,1024]{2,1,0:T(8,128)S(1)} %bitcast.7, f32[4,8,1024]{2,1,0:T(8,128)S(1)} %bitcast.8, f32[4,8,1024]{2,1,0:T(8,128)S(1)} %bitcast.9, ...), custom_call_target="tpu_custom_call" | custom-call | tf_op jit(solution)/shard_map/pallas_call | solution.py:283
  54.2 0.7 %copy.13 = f32[1,4,8,1024]{3,2,1,0:T(8,128)} copy(f32[1,4,8,1024]{3,2,1,0:T(8,128)S(1)} %bitcast.12) | data formatting | bytes 262144
  54.9 0.7 %copy.14 = f32[1,4,8,1024]{3,2,1,0:T(8,128)} copy(f32[1,4,8,1024]{3,2,1,0:T(8,128)S(1)} %bitcast.11) | data formatting | bytes 262144
  55.5 0.7 %copy.15 = f32[1,4,8,1024]{3,2,1,0:T(8,128)} copy(f32[1,4,8,1024]{3,2,1,0:T(8,128)S(1)} %bitcast.10) | data formatting | bytes 262144
Async XLA Ops:
  1.3 0.7 %copy-start.3 = (s32[1,8,16]{2,1,0:T(8,128)S(1)}, s32[1,8,16]{2,1,0:T(8,128)}, u32[]{:S(2)}) copy-start(s32[1,8,16]{2,1,0:T(8,128)} %param.9) | copy-start | bytes 1540
  1.3 0.7 %copy-start.4 = (s32[8]{0:T(128)S(1)}, s32[8]{0:T(128)}, u32[]{:S(2)}) copy-start(s32[8]{0:T(128)} %pairs.1) | copy-start | bytes 100
  2.0 0.9 %copy-start = (f32[1,4,8,1024]{3,2,1,0:T(8,128)S(1)}, f32[1,4,8,1024]{3,2,1,0:T(8,128)}, u32[]{:S(2)}) copy-start(f32[1,4,8,1024]{3,2,1,0:T(8,128)} %param.6) | copy-start | bytes 393220
  2.9 0.9 %copy-start.1 = (f32[1,4,8,1024]{3,2,1,0:T(8,128)S(1)}, f32[1,4,8,1024]{3,2,1,0:T(8,128)}, u32[]{:S(2)}) copy-start(f32[1,4,8,1024]{3,2,1,0:T(8,128)} %param.7) | copy-start | bytes 393220
  3.8 0.9 %copy-start.2 = (f32[1,4,8,1024]{3,2,1,0:T(8,128)S(1)}, f32[1,4,8,1024]{3,2,1,0:T(8,128)}, u32[]{:S(2)}) copy-start(f32[1,4,8,1024]{3,2,1,0:T(8,128)} %param.8) | copy-start | bytes 393220

commit v3 on v2

--- a/solution.py
+++ b/solution.py
@@ -27,11 +27,15 @@
 
 
 def steps_kernel(
-    n, pairs, rotation, ax, az, ra, drag, ax_out, az_out, ra_out,
-    mid, pred, wide, diag, tell_a, hear_a, tell_b, hear_b, sums, plane, got, inflow, landing,
-    send_a, recv_a, send_b, recv_b, send_s, recv_s, send_p, recv_p, send_x, recv_x,
+    n, pairs, rotation, ax_in, az_in, ra_in, drag, ax_out, az_out, ra_out,
+    held, mid, pred, wide, diag, tell_a, hear_a, tell_b, hear_b, folds, sums, plane, got, inflow, landing,
+    send_a, recv_a, send_b, recv_b, send_s, recv_s, send_p, recv_p, send_x, recv_x, load_sem,
 ):
-    layers, rows, cells = ax.shape
+    layers, rows, cells = ax_in.shape
+    ax, az, ra = (held.at[f] for f in range(3))
+    loads = [pltpu.make_async_copy(src, held.at[f], load_sem.at[f]) for f, src in enumerate((ax_in, az_in, ra_in))]
+    for load in loads:
+        load.start()
     stages = got.shape[0]
     me = lax.axis_index("az")
     sleeve = lax.axis_index("sec") == 1
@@ -57,6 +61,9 @@
         spread = jnp.where(lane // block_cells == block, flags[:, block : block + 1], spread)
     diag[...] = jnp.zeros_like(diag)
     diag[0:rows, :] = 4.0 + diagonal_add - centre + drag_rate * spread
+
+    for load in loads:
+        load.wait()
 
     def exchange(tell, hear, send, recv):
         copies = []
@@ -216,8 +223,14 @@
             c_b2 = c_diag[0:rows] * b2 - 2.0 * (next_row + next_cell)
             parts = (b0 * b0, b0 * b1, b1 * b1, b1 * b2, b2 * b2, b2 * c_b2)
             for k, part in enumerate(parts):
-                ss[me, k, l : l + 1, :] = total(part)
+                folds[k, l : l + 1, :] = total(part)
             basis.append((v1, v2))
+
+        slot = lax.broadcasted_iota(jnp.int32, (layers, 128), 1)
+        packed = jnp.zeros((layers, 128), jnp.float32)
+        for k in range(6):
+            packed = jnp.where(slot == k, jnp.sum(folds[k], axis=1, keepdims=True), packed)
+        ss[me] = packed
 
         def sum_copy(k, slot_of):
             return pltpu.make_async_remote_copy(
@@ -239,7 +252,7 @@
         lax.fori_loop(1, n, take, 0)
 
         moments = lax.fori_loop(1, n, lambda j, acc: acc + ss[j], ss[0])
-        m = [jnp.sum(moments[k], axis=1, keepdims=True) for k in range(6)]
+        m = [moments[:, k : k + 1] for k in range(6)]
         g = [m[k + 1] + centre * m[k] for k in range(5)]
         inv0 = 1.0 / g[0]
         l10, l20 = g[1] * inv0, g[2] * inv0
@@ -283,9 +296,10 @@
     return pl.pallas_call(
         functools.partial(steps_kernel, n),
         out_shape=(field, field, field),
-        in_specs=[smem, smem] + [vmem] * 4,
+        in_specs=[smem, smem] + [pl.BlockSpec(memory_space=pltpu.HBM)] * 3 + [vmem],
         out_specs=(vmem,) * 3,
         scratch_shapes=[
+            pltpu.VMEM((3, layers, rows, cells), f32),
             pltpu.VMEM((3, layers, rows, cells), f32),
             pltpu.VMEM((3, layers, rows, cells), f32),
             pltpu.VMEM((layers, 2 * rows, cells), f32),
@@ -294,7 +308,8 @@
             pltpu.VMEM((STEPS, 2, told, cells), f32),
             pltpu.VMEM((STEPS, 2, 4 * layers, cells), f32),
             pltpu.VMEM((STEPS, 2, 4 * layers, cells), f32),
-            pltpu.VMEM((STEPS, n, 6, layers, 128), f32),
+            pltpu.VMEM((6, layers, 128), f32),
+            pltpu.VMEM((STEPS, n, layers, 128), f32),
             pltpu.VMEM((stages + 1, 3, rows, cells), f32),
             pltpu.VMEM((stages, 3, rows, cells), f32),
             pltpu.VMEM((3, rows, cells), f32),
@@ -309,9 +324,10 @@
             dma((stages, 3)),
             dma((2, 3)),
             dma((2, 3)),
+            dma((3,)),
         ],
         compiler_params=pltpu.CompilerParams(
-            collective_id=0, has_side_effects=True, vmem_limit_bytes=32 * 1024 * 1024
+            collective_id=0, has_side_effects=True, vmem_limit_bytes=60 * 1024 * 1024
         ),
     )(pairs, rotation, ax, az, ra, drag)
 

time: 56.4 us -> 53.7 us (0.952)
  local copies, waits for them, and re-layouts: 5.35 us -> 3.21 us
  Pallas kernels: 49.5 us -> 48.9 us
    unnamed x13 -> x7, local copies, waits for them, and re-layouts: 5.35 us -> 3.21 us
    pallas_call x1, Pallas kernels: 49.5 us -> 48.9 us  [steps(): pl.pallas_call(functools.partial(steps_kernel, n), out_shape=(field, fiel...]
where the time goes in v3:
time: 53.7 us; the launch traced here: 53.4 us
  Pallas kernels  48.9 us (91%)
  local copies, waits for them, and re-layouts  3.21 us (6%)
  between operations  1.3 us (2%)
    pallas_call x1, Pallas kernels, steps(): pl.pallas_call(functools.partial(steps_kernel, n), out_shape=(field, fiel...  48.9 us
    unnamed x7, local copies, waits for them, and re-layouts  3.21 us

profile of v3, /device:TPU:3, one launch (start us, length us, event | category | flops | bytes accessed | tf_op | source)
XLA Modules:
  0.0 53.4 jit_solution(9405417764098345784)
XLA Ops:
  1.3 48.9 %shard_map.85 = (f32[4,8,1024]{2,1,0:T(8,128)}, f32[4,8,1024]{2,1,0:T(8,128)}, f32[4,8,1024]{2,1,0:T(8,128)}) custom-call(s32[8]{0:T(128)} %pairs.1, s32[1]{0:T(128)S(6)} %copy.12.rotation, f32[4,8,1024]{2,1,0:T(8,128)} %bitcast.7, f32[4,8,1024]{2,1,0:T(8,128)} %bitcast.8, f32[4,8,1024]{2,1,0:T(8,128)} %bitcast.9, s32[8,16]{1,0:T(8,128)} %bitcast.13), custom_call_target="tpu_custom_call" | custom-call | tf_op jit(solution)/shard_map/pallas_call | solution.py:296
  50.2 0.0 copy-start.1
  50.2 1.6 %copy.13 = f32[1,4,8,1024]{3,2,1,0:T(8,128)} copy(f32[1,4,8,1024]{3,2,1,0:T(8,128)} %bitcast.12) | data formatting | bytes 262144
  51.8 0.0 copy-done.1
  51.8 0.0 copy-start
  51.8 0.7 %copy.14 = f32[1,4,8,1024]{3,2,1,0:T(8,128)} copy(f32[1,4,8,1024]{3,2,1,0:T(8,128)S(1)} %bitcast.11) | data formatting | bytes 262144
  52.5 0.3 copy-done
  52.8 0.7 %copy.15 = f32[1,4,8,1024]{3,2,1,0:T(8,128)} copy(f32[1,4,8,1024]{3,2,1,0:T(8,128)S(1)} %bitcast.10) | data formatting | bytes 262144
Async XLA Ops:
  50.2 1.6 %copy-start.1 = (f32[4,8,1024]{2,1,0:T(8,128)S(1)}, f32[4,8,1024]{2,1,0:T(8,128)}, u32[]{:S(2)}) copy-start(f32[4,8,1024]{2,1,0:T(8,128)} %get-tuple-element.7) | copy-start | bytes 393220
  51.8 1.0 %copy-start = (f32[4,8,1024]{2,1,0:T(8,128)S(1)}, f32[4,8,1024]{2,1,0:T(8,128)}, u32[]{:S(2)}) copy-start(f32[4,8,1024]{2,1,0:T(8,128)} %get-tuple-element.8) | copy-start | bytes 393220
